TPU v7x, 256 devices: a whole 4x4x8 slice. The times are simulated.
256 devices in a mesh: bx: 16 (over z, core), by: 16 (over x, y).
Axes of the slice: x: 4, y: 4, z: 8, core: 2. Of those that a mesh axis runs over, the one named last changes fastest.
Arguments:
- density: bfloat16 [16, 16, 16, 64, 4096], P('bx', 'by'), may hold values from -5 to 5
- inner_order: int32 [16], replicated, may hold values from 0 to 15, each once
- outer_order: int32 [16], replicated, may hold values from 0 to 15, each once
- footprints: int32 [16, 16, 4], P('bx', 'by'), may hold values from 0 to 4096, as said below
Outputs:
- composite: float32 [4, 64, 4096], P(None, None, 'bx')
Inputs may be any that keep to these rules, and one draw needn't show every extreme that they name: footprints[i, j] holds first row, end row, first column and end column of brick (i, j)'s rectangle, first below end; rows lie in 0 to 64; one brick's rectangle is the whole band.
All inputs are finite; a program needn't handle non-finite values.
Results may differ from a plain program's by a relative error of at most 0.0005.
Values may be sent and summed in bfloat16 or wider, within the bound.
A program may use at most 128 MiB of HBM per device.

v0:
```python
import functools

import jax
import jax.numpy as jnp
from jax import lax
from jax.experimental import pallas as pl
from jax.experimental.pallas import tpu as pltpu
from jax.sharding import PartitionSpec as P

MESH = pl.DeviceIdType.MESH
LOG2E = 1.4426950408889634
STRIP = 16
CUTS = 2
FIRST = 2
CODE = 65534.0


def encode(value):
    root = lax.rsqrt(lax.rsqrt(jnp.clip(value, 0.0, 1.0)))
    return (root * CODE + 0.5).astype(jnp.int32).astype(jnp.uint16)


def decode(code):
    root = code.astype(jnp.int32).astype(jnp.float32)
    square = root * root * (1.0 / (CODE * CODE))
    return square * square


def march(load, depth, extinct):
    transmit = tanhs = green = None
    for sample in range(depth):
        values = load(sample).astype(jnp.float32)
        square = values * values
        bend = jnp.minimum((2.5 - values) * (2.0 * LOG2E), 0.0)
        survive = jnp.exp2(square * (-extinct * LOG2E) + bend)
        bell = jnp.exp2(square * (-0.5 * LOG2E))
        slope = jnp.tanh(values)
        if sample == 0:
            left = survive
            weight = 1.0 - survive
            tanhs = weight * slope
            green = weight * bell
        else:
            left = transmit * survive
            weight = transmit - left
            tanhs = tanhs + weight * slope
            green = green + weight * bell
        transmit = left
    opaque = 1.0 - transmit
    return 0.5 * (opaque + tanhs), green, 0.5 * (opaque - tanhs)


def blend(images, order_ref, count, width):
    red = green = blue = through = None
    for rank in range(count):
        at = order_ref[rank]
        r, g, b = (images[at, channel, :, :width] for channel in range(3))
        clear = 1.0 - (r + b)
        if rank == 0:
            red, green, blue, through = r, g, b, clear
        else:
            red = red + through * r
            green = green + through * g
            blue = blue + through * b
            through = through * clear
    return red, green, blue


def kernel(
    sizes,
    extinct,
    inner_hbm,
    outer_hbm,
    bounds_hbm,
    density_ref,
    out_ref,
    result,
    slab,
    sending,
    landed,
    groups,
    images,
    inner_ref,
    outer_ref,
    bounds_ref,
    inner_inverse,
    outer_inverse,
    small_sem,
    load_sem,
    send_sem,
    recv_sem,
    group_send_sem,
    group_recv_sem,
    out_sem,
):
    across_x, across_y, side, depth, rows, columns = sizes
    chips = across_x // 2
    block = columns // across_x
    strips = rows // STRIP
    cut = block // CUTS
    last = strips - 1
    pieces = [(strip, 0, block) for strip in range(last)]
    pieces += [(last, cut * at, cut) for at in range(CUTS)]
    i = lax.axis_index("bx")
    j = lax.axis_index("by")
    z, core = lax.div(i, 2), lax.rem(i, 2)
    x, y = lax.div(j, side), lax.rem(j, side)

    def column_peer(n):
        step = n % chips
        hops = chips // 2 + (1 - 2 * (step % 2)) * ((step + 1) // 2)
        return lax.rem(z + hops, chips) * 2 + lax.rem(core + 1 - n // chips, 2)

    def far(k):
        return 2 - k + 3 * (k // 2) - 2 * ((k + 1) // 4)

    def group_peer(n):
        return lax.rem(x + far(n // side), side) * side + lax.rem(y + far(n % side), side)

    def load(strip):
        return pltpu.make_async_copy(
            density_ref.at[0, 0, :, pl.ds(pl.multiple_of(strip * STRIP, STRIP), STRIP), :],
            slab.at[strip],
            load_sem.at[strip],
        )

    def remote(src, dst, sends, recvs, device):
        return pltpu.make_async_remote_copy(
            src_ref=src, dst_ref=dst, send_sem=sends, recv_sem=recvs, device_id=device, device_id_type=MESH
        )

    def view(buffer, piece, at):
        strip, left, width = piece
        return buffer.at[strip, at, :, :, pl.ds(left, width)]

    def number(piece):
        strip, left, width = piece
        return strip + left // width

    def column_copy(piece, n, slot):
        return remote(
            view(sending, piece, n),
            view(landed, piece, slot),
            send_sem.at[number(piece), n],
            recv_sem.at[number(piece), slot],
            (column_peer(n), j),
        )

    def group_copy(piece, n, slot):
        return remote(
            view(groups, piece, j),
            view(groups, piece, slot),
            group_send_sem.at[number(piece), n],
            group_recv_sem.at[number(piece), slot],
            (i, group_peer(n)),
        )

    def out_copy(piece):
        strip, left, width = piece
        where = (slice(None), pl.ds(strip * STRIP, STRIP), pl.ds(left, width))
        return pltpu.make_async_copy(result.at[where], out_ref.at[where], out_sem.at[number(piece)])

    def each(count, act, first=0, flat=False):
        if flat:
            for n in range(first, count):
                act(n)
            return

        def step(n, carry):
            act(n)
            return carry

        lax.fori_loop(first, count, step, 0)

    def render(piece, n):
        strip, at, width = piece
        left = pl.multiple_of(column_peer(n) * block + at, width)
        colours = march(lambda s: slab[strip, s, :, pl.ds(left, width)], depth, extinct)
        row = lax.broadcasted_iota(jnp.int32, (STRIP, width), 0) + strip * STRIP
        column = lax.broadcasted_iota(jnp.int32, (STRIP, width), 1) + left
        inside = (
            (row >= bounds_ref[0, 0, 0])
            & (row < bounds_ref[0, 0, 1])
            & (column >= bounds_ref[0, 0, 2])
            & (column < bounds_ref[0, 0, 3])
        )
        return [encode(jnp.where(inside, colour, 0.0)) for colour in colours]

    def put(buffer, piece, at, codes):
        strip, left, width = piece
        for channel, code in enumerate(codes):
            buffer[strip, at, channel, :, pl.ds(left, width)] = code

    def render_send(piece, n):
        put(sending, piece, n, render(piece, n))

    def render_keep(piece):
        put(landed, piece, i, render(piece, across_x - 1))

    def render_and_send(piece, n):
        render_send(piece, n)
        column_copy(piece, n, i).start()

    def take(buffer, piece, at):
        strip, left, width = piece
        for channel in range(3):
            images[at, channel, :, :width] = decode(buffer[strip, at, channel, :, pl.ds(left, width)])

    def finish(piece):
        strip, left, width = piece
        take(groups, piece, j)

        def arrive(n):
            peer = group_peer(n)
            group_copy(piece, n, peer).wait_recv()
            take(groups, piece, peer)

        each(across_y - 1, arrive, 0, piece is pieces[-1])
        red, green, blue = blend(images, outer_inverse, across_y, width)
        for channel, colour in enumerate((red, green, blue, red + blue)):
            result[channel, pl.ds(strip * STRIP, STRIP), pl.ds(left, width)] = colour
        out_copy(piece).start()

    def drain_column(piece):
        each(across_x - 1, lambda n: column_copy(piece, n, i).wait_send())

    def drain_group(piece):
        each(across_y - 1, lambda n: group_copy(piece, n, j).wait_send(), 0, piece is pieces[-1])

    small = [
        pltpu.make_async_copy(inner_hbm, inner_ref, small_sem.at[0]),
        pltpu.make_async_copy(outer_hbm, outer_ref, small_sem.at[1]),
        pltpu.make_async_copy(bounds_hbm, bounds_ref, small_sem.at[2]),
    ]
    small[2].start()
    load(0).start()

    barrier = pltpu.get_barrier_semaphore()

    def greet_column(n):
        pl.semaphore_signal(barrier, inc=1, device_id=(column_peer(n), j), device_id_type=MESH)

    def greet_group(n):
        pl.semaphore_signal(barrier, inc=1, device_id=(i, group_peer(n)), device_id_type=MESH)

    each(across_x - 1, greet_column, 0, True)
    each(across_y - 1, greet_group, 0, True)

    each(strips, lambda strip: load(strip).start(), 1)
    small[0].start()
    small[1].start()
    small[2].wait()
    load(0).wait()
    each(FIRST, lambda n: render_send(pieces[0], n))
    pl.semaphore_wait(barrier, across_x - 1 + across_y - 1)
    each(FIRST, lambda n: column_copy(pieces[0], n, i).start())
    each(across_x - 1, lambda n: render_and_send(pieces[0], n), FIRST)
    render_keep(pieces[0])

    def follow(strip):
        piece = (strip, 0, block)
        load(strip).wait()
        each(across_x - 1, lambda n: render_and_send(piece, n))
        render_keep(piece)

    each(last, follow, 1)
    load(last).wait()
    for piece in pieces[last:]:
        each(across_x - 1, lambda n: render_and_send(piece, n))
        render_keep(piece)

    def invert(order_ref, inverse_ref, count):
        def one(rank):
            found = jnp.int32(0)
            for at in range(count):
                found = jnp.where(order_ref[at] == rank, at, found)
            inverse_ref[rank] = found

        each(count, one)

    small[0].wait()
    small[1].wait()
    invert(inner_ref, inner_inverse, across_x)
    invert(outer_ref, outer_inverse, across_y)

    def advance(piece):
        take(landed, piece, i)

        def arrive(n):
            peer = column_peer(n)
            column_copy(piece, n, peer).wait_recv()
            take(landed, piece, peer)

        each(across_x - 1, arrive, 0, piece is pieces[-1])
        width = piece[2]
        put(groups, piece, j, [encode(c) for c in blend(images, inner_inverse, across_x, width)])
        each(across_y - 1, lambda n: group_copy(piece, n, j).start(), 0, piece is pieces[-1])

    advance(pieces[0])
    for before, piece in zip(pieces[:-1], pieces[1:]):
        advance(piece)
        finish(before)
        drain_column(before)
        drain_group(before)
    drain_column(pieces[-1])
    finish(pieces[-1])
    drain_group(pieces[-1])
    for piece in pieces:
        out_copy(piece).wait()


def on_device(density, inner_order, outer_order, footprints):
    across_x = lax.axis_size("bx")
    across_y = lax.axis_size("by")
    depth, rows, columns = density.shape[2:]
    extinct = 1.5 / (across_x * across_y * depth)
    side = 1
    while side * side < across_y:
        side *= 2
    block = columns // across_x
    strips = rows // STRIP
    pieces = strips - 1 + CUTS
    strip_shape = (3, STRIP, block)
    hbm = pl.BlockSpec(memory_space=pltpu.HBM)
    return pl.pallas_call(
        functools.partial(kernel, (across_x, across_y, side, depth, rows, columns), extinct),
        out_shape=jax.ShapeDtypeStruct((4, rows, block), jnp.float32),
        in_specs=[hbm] * 4,
        out_specs=hbm,
        scratch_shapes=[
            pltpu.VMEM((4, rows, block), jnp.float32),
            pltpu.VMEM((strips, depth, STRIP, columns), jnp.bfloat16),
            pltpu.VMEM((strips, across_x - 1) + strip_shape, jnp.uint16),
            pltpu.VMEM((strips, across_x) + strip_shape, jnp.uint16),
            pltpu.VMEM((strips, across_y) + strip_shape, jnp.uint16),
            pltpu.VMEM((max(across_x, across_y),) + strip_shape, jnp.float32),
            pltpu.SMEM((across_x,), jnp.int32),
            pltpu.SMEM((across_y,), jnp.int32),
            pltpu.SMEM((1, 1, 4), jnp.int32),
            pltpu.SMEM((across_x,), jnp.int32),
            pltpu.SMEM((across_y,), jnp.int32),
            pltpu.SemaphoreType.DMA((3,)),
            pltpu.SemaphoreType.DMA((strips,)),
            pltpu.SemaphoreType.DMA((pieces, across_x)),
            pltpu.SemaphoreType.DMA((pieces, across_x)),
            pltpu.SemaphoreType.DMA((pieces, across_y)),
            pltpu.SemaphoreType.DMA((pieces, across_y)),
            pltpu.SemaphoreType.DMA((pieces,)),
        ],
        compiler_params=pltpu.CompilerParams(
            collective_id=0, has_side_effects=True, vmem_limit_bytes=60 << 20
        ),
    )(inner_order, outer_order, footprints, density)


def solution(mesh):
    in_specs = (P("bx", "by", None, None, None), P(), P(), P("bx", "by", None))
    out_specs = P(None, None, "bx")
    return jax.shard_map(
        on_device, mesh=mesh, in_specs=in_specs, out_specs=out_specs, check_vma=False
    )
```

profile of v0, /device:TPU:1, one launch (start us, length us, event | category | flops | bytes accessed | tf_op | source)
XLA Modules:
  0.0 55.6 jit_solution(16258296370831947799)
XLA Ops:
  0.0 54.0 %shard_map.46 = f32[4,64,256]{2,1,0:T(8,128)} custom-call(s32[16]{0:T(128)} %inner_hbm.1, s32[16]{0:T(128)} %outer_hbm.1, s32[1,1,4]{2,1,0:T(1,128)} %bounds_hbm.1, bf16[1,1,16,64,4096]{4,3,2,1,0:T(8,128)(2,1)} %density_ref.1), custom_call_target="tpu_custom_call" | custom-call | tf_op jit(solution)/shard_map/pallas_call | solution.py:325
  54.0 1.7 %copy.6 = f32[4,64,256]{2,1,0:T(8,128)} copy(f32[4,64,256]{2,1,0:T(8,128)} %shard_map.46) | data formatting | bytes 524288
where the time goes:
time: 55.7 us; the launch traced here: 55.6 us
  Pallas kernels  54 us (97%)
  local copies, waits for them, and re-layouts  1.67 us (3%)
    pallas_call x1, Pallas kernels, on_device(): pl.pallas_call(functools.partial(kernel, (across_x, across_y, side, depth...  54 us
    unnamed x1, local copies, waits for them, and re-layouts  1.67 us

commit v1 on v0

--- a/solution.py
+++ b/solution.py
@@ -69,20 +69,15 @@
 def kernel(
     sizes,
     extinct,
-    inner_hbm,
-    outer_hbm,
-    bounds_hbm,
+    small_hbm,
     density_ref,
     out_ref,
-    result,
     slab,
     sending,
     landed,
     groups,
     images,
-    inner_ref,
-    outer_ref,
-    bounds_ref,
+    small_ref,
     inner_inverse,
     outer_inverse,
     small_sem,
@@ -91,7 +86,6 @@
     recv_sem,
     group_send_sem,
     group_recv_sem,
-    out_sem,
 ):
     across_x, across_y, side, depth, rows, columns = sizes
     chips = across_x // 2
@@ -155,11 +149,6 @@
             (i, group_peer(n)),
         )
 
-    def out_copy(piece):
-        strip, left, width = piece
-        where = (slice(None), pl.ds(strip * STRIP, STRIP), pl.ds(left, width))
-        return pltpu.make_async_copy(result.at[where], out_ref.at[where], out_sem.at[number(piece)])
-
     def each(count, act, first=0, flat=False):
         if flat:
             for n in range(first, count):
@@ -179,10 +168,10 @@
         row = lax.broadcasted_iota(jnp.int32, (STRIP, width), 0) + strip * STRIP
         column = lax.broadcasted_iota(jnp.int32, (STRIP, width), 1) + left
         inside = (
-            (row >= bounds_ref[0, 0, 0])
-            & (row < bounds_ref[0, 0, 1])
-            & (column >= bounds_ref[0, 0, 2])
-            & (column < bounds_ref[0, 0, 3])
+            (row >= small_ref[across_x + across_y])
+            & (row < small_ref[across_x + across_y + 1])
+            & (column >= small_ref[across_x + across_y + 2])
+            & (column < small_ref[across_x + across_y + 3])
         )
         return [encode(jnp.where(inside, colour, 0.0)) for colour in colours]
 
@@ -218,8 +207,7 @@
         each(across_y - 1, arrive, 0, piece is pieces[-1])
         red, green, blue = blend(images, outer_inverse, across_y, width)
         for channel, colour in enumerate((red, green, blue, red + blue)):
-            result[channel, pl.ds(strip * STRIP, STRIP), pl.ds(left, width)] = colour
-        out_copy(piece).start()
+            out_ref[channel, pl.ds(strip * STRIP, STRIP), pl.ds(left, width)] = colour
 
     def drain_column(piece):
         each(across_x - 1, lambda n: column_copy(piece, n, i).wait_send())
@@ -228,11 +216,9 @@
         each(across_y - 1, lambda n: group_copy(piece, n, j).wait_send(), 0, piece is pieces[-1])
 
     small = [
-        pltpu.make_async_copy(inner_hbm, inner_ref, small_sem.at[0]),
-        pltpu.make_async_copy(outer_hbm, outer_ref, small_sem.at[1]),
-        pltpu.make_async_copy(bounds_hbm, bounds_ref, small_sem.at[2]),
+        pltpu.make_async_copy(small_hbm, small_ref, small_sem.at[0]),
     ]
-    small[2].start()
+    small[0].start()
     load(0).start()
 
     barrier = pltpu.get_barrier_semaphore()
@@ -247,9 +233,7 @@
     each(across_y - 1, greet_group, 0, True)
 
     each(strips, lambda strip: load(strip).start(), 1)
-    small[0].start()
-    small[1].start()
-    small[2].wait()
+    small[0].wait()
     load(0).wait()
     each(FIRST, lambda n: render_send(pieces[0], n))
     pl.semaphore_wait(barrier, across_x - 1 + across_y - 1)
@@ -269,19 +253,17 @@
         each(across_x - 1, lambda n: render_and_send(piece, n))
         render_keep(piece)
 
-    def invert(order_ref, inverse_ref, count):
+    def invert(order_at, inverse_ref, count):
         def one(rank):
             found = jnp.int32(0)
             for at in range(count):
-                found = jnp.where(order_ref[at] == rank, at, found)
+                found = jnp.where(small_ref[order_at + at] == rank, at, found)
             inverse_ref[rank] = found
 
         each(count, one)
 
-    small[0].wait()
-    small[1].wait()
-    invert(inner_ref, inner_inverse, across_x)
-    invert(outer_ref, outer_inverse, across_y)
+    invert(0, inner_inverse, across_x)
+    invert(across_x, outer_inverse, across_y)
 
     def advance(piece):
         take(landed, piece, i)
@@ -305,8 +287,6 @@
     drain_column(pieces[-1])
     finish(pieces[-1])
     drain_group(pieces[-1])
-    for piece in pieces:
-        out_copy(piece).wait()
 
 
 def on_device(density, inner_order, outer_order, footprints):
@@ -325,18 +305,15 @@
     return pl.pallas_call(
         functools.partial(kernel, (across_x, across_y, side, depth, rows, columns), extinct),
         out_shape=jax.ShapeDtypeStruct((4, rows, block), jnp.float32),
-        in_specs=[hbm] * 4,
-        out_specs=hbm,
+        in_specs=[pl.BlockSpec(memory_space=pl.ANY), hbm],
+        out_specs=pl.BlockSpec(memory_space=pltpu.VMEM),
         scratch_shapes=[
-            pltpu.VMEM((4, rows, block), jnp.float32),
             pltpu.VMEM((strips, depth, STRIP, columns), jnp.bfloat16),
             pltpu.VMEM((strips, across_x - 1) + strip_shape, jnp.uint16),
             pltpu.VMEM((strips, across_x) + strip_shape, jnp.uint16),
             pltpu.VMEM((strips, across_y) + strip_shape, jnp.uint16),
             pltpu.VMEM((max(across_x, across_y),) + strip_shape, jnp.float32),
-            pltpu.SMEM((across_x,), jnp.int32),
-            pltpu.SMEM((across_y,), jnp.int32),
-            pltpu.SMEM((1, 1, 4), jnp.int32),
+            pltpu.SMEM((across_x + across_y + 4,), jnp.int32),
             pltpu.SMEM((across_x,), jnp.int32),
             pltpu.SMEM((across_y,), jnp.int32),
             pltpu.SemaphoreType.DMA((3,)),
@@ -345,12 +322,11 @@
             pltpu.SemaphoreType.DMA((pieces, across_x)),
             pltpu.SemaphoreType.DMA((pieces, across_y)),
             pltpu.SemaphoreType.DMA((pieces, across_y)),
-            pltpu.SemaphoreType.DMA((pieces,)),
         ],
         compiler_params=pltpu.CompilerParams(
-            collective_id=0, has_side_effects=True, vmem_limit_bytes=60 << 20
+            collective_id=0, has_side_effects=True, vmem_limit_bytes=50 << 20
         ),
-    )(inner_order, outer_order, footprints, density)
+    )(jnp.concatenate([inner_order, outer_order, footprints[0, 0]]), density)
 
 
 def solution(mesh):

time: 55.7 us -> 54.8 us (0.984)
  local copies, waits for them, and re-layouts: 1.67 us -> 0.71 us
  Pallas kernels: 54 us -> 53.2 us
  other arithmetic: 0 us -> 0.76 us
    unnamed x1, local copies, waits for them, and re-layouts: 1.67 us -> 0.71 us
    concatenate x0 -> x1, other arithmetic: none -> 0.76 us  [on_device(): jnp.concatenate([inner_order, outer_order, footprints[0, 0]])]
    pallas_call x1, Pallas kernels: 54 us -> 53.2 us  [on_device(): pl.pallas_call(functools.partial(kernel, (across_x, across_y, side, depth...]
where the time goes in v1:
time: 54.8 us; the launch traced here: 54.7 us
  Pallas kernels  53.2 us (97%)
  other arithmetic  0.76 us (1%)
  local copies, waits for them, and re-layouts  0.71 us (1%)
    pallas_call x1, Pallas kernels, on_device(): pl.pallas_call(functools.partial(kernel, (across_x, across_y, side, depth...  53.2 us

profile of v1, /device:TPU:1, one launch (start us, length us, event | category | flops | bytes accessed | tf_op | source)
XLA Modules:
  0.0 54.7 jit_solution(4428462339337639732)
XLA Ops:
  0.0 0.8 %pad_add_fusion.small_hbm = s32[36]{0:T(128)S(1)} fusion(s32[4]{0:T(128)} %bitcast.1, s32[16]{0:T(128)} %param.6, s32[16]{0:T(128)} %param.5), kind=kLoop, calls=%fused_computation | loop fusion | flops 72 | bytes 288 | tf_op jit(solution)/shard_map/concatenate | solution.py:329
  0.8 53.2 %shard_map.46 = f32[4,64,256]{2,1,0:T(8,128)S(1)} custom-call(s32[36]{0:T(128)S(1)} %pad_add_fusion.small_hbm, bf16[1,1,16,64,4096]{4,3,2,1,0:T(8,128)(2,1)} %density_ref.1), custom_call_target="tpu_custom_call" | custom-call | tf_op jit(solution)/shard_map/pallas_call | solution.py:305
  54.0 0.7 %copy.6 = f32[4,64,256]{2,1,0:T(8,128)} copy(f32[4,64,256]{2,1,0:T(8,128)S(1)} %shard_map.46) | data formatting | bytes 524288

commit v2 on v1

--- a/solution.py
+++ b/solution.py
@@ -285,8 +285,8 @@
         drain_column(before)
         drain_group(before)
     drain_column(pieces[-1])
+    drain_group(pieces[-1])
     finish(pieces[-1])
-    drain_group(pieces[-1])
 
 
 def on_device(density, inner_order, outer_order, footprints):

time: 54.8 us -> 54.8 us (level)
  no operation moved by 1% of the time
where the time goes in v2:
time: 54.8 us; the launch traced here: 54.7 us
  Pallas kernels  53.2 us (97%)
  other arithmetic  0.76 us (1%)
  local copies, waits for them, and re-layouts  0.71 us (1%)
    pallas_call x1, Pallas kernels, on_device(): pl.pallas_call(functools.partial(kernel, (across_x, across_y, side, depth...  53.2 us

profile of v2, /device:TPU:1, one launch (start us, length us, event | category | flops | bytes accessed | tf_op | source)
XLA Modules:
  0.0 54.7 jit_solution(10834741285378076250)
XLA Ops:
  0.0 0.8 %pad_add_fusion.small_hbm = s32[36]{0:T(128)S(1)} fusion(s32[4]{0:T(128)} %bitcast.1, s32[16]{0:T(128)} %param.6, s32[16]{0:T(128)} %param.5), kind=kLoop, calls=%fused_computation | loop fusion | flops 72 | bytes 288 | tf_op jit(solution)/shard_map/concatenate | solution.py:329
  0.8 53.2 %shard_map.46 = f32[4,64,256]{2,1,0:T(8,128)S(1)} custom-call(s32[36]{0:T(128)S(1)} %pad_add_fusion.small_hbm, bf16[1,1,16,64,4096]{4,3,2,1,0:T(8,128)(2,1)} %density_ref.1), custom_call_target="tpu_custom_call" | custom-call | tf_op jit(solution)/shard_map/pallas_call | solution.py:305
  54.0 0.7 %copy.6 = f32[4,64,256]{2,1,0:T(8,128)} copy(f32[4,64,256]{2,1,0:T(8,128)S(1)} %shard_map.46) | data formatting | bytes 524288
